TPU v7x, 32 devices: a whole 2x2x4 slice. The times are simulated.
32 devices in a mesh: groups: 2 (over y), res: 16 (over z, x, core), feat: 1.
Axes of the slice: x: 2, y: 2, z: 4, core: 2. Of those that a mesh axis runs over, the one named last changes fastest.
Arguments:
- node_feats: bfloat16 [2048, 512], P(('groups', 'res')), parts along dimension 0, may hold values from -6 to 6
- edge_feats: bfloat16 [2048, 20, 256], P(('groups', 'res')), parts along dimension 0, may hold values from -6 to 6
- neighbours: int32 [2048, 20], P(('groups', 'res')), parts along dimension 0, may hold values from 0 to 1023, as said below
- w_self: bfloat16 [512, 256], P(None, 'feat'), may hold values from -0.25 to 0.25
- w_nbr: bfloat16 [512, 256], P(None, 'feat'), may hold values from -0.25 to 0.25
- w_edge: bfloat16 [256, 256], P(None, 'feat'), may hold values from -0.375 to 0.375
- bias: float32 [256], P('feat'), may hold values from -3 to 3
- w_edge_out: bfloat16 [256, 256], P('feat'), may hold values from -0.375 to 0.375
- w_node_out: bfloat16 [256, 512], P('feat'), may hold values from -0.375 to 0.375
- grad_nodes: bfloat16 [2048, 512], P(('groups', 'res')), parts along dimension 0, may hold values from -6 to 6
- grad_edges: bfloat16 [2048, 20, 256], P(('groups', 'res')), parts along dimension 0, may hold values from -6 to 6
Outputs:
- d_nodes: bfloat16 [2048, 512], P(('groups', 'res'), 'feat'), parts along dimension 0
- d_edges: bfloat16 [2048, 20, 256], P(('groups', 'res'), None, 'feat'), parts along dimension 0
- d_self: bfloat16 [1024, 256], P('groups', 'feat'), parts along dimension 0
- d_nbr: bfloat16 [1024, 256], P('groups', 'feat'), parts along dimension 0
- d_edge_in: bfloat16 [512, 256], P('groups', 'feat'), parts along dimension 0
- d_bias: float32 [512], P(('groups', 'feat')), parts along dimension 0
- d_edge_out: bfloat16 [512, 256], P(('groups', 'feat')), parts along dimension 0
- d_node_out: bfloat16 [512, 512], P(('groups', 'feat')), parts along dimension 0
There are 2 independent parts, one for each index of `groups`. A program takes and returns all parts, laid end to end along the dimension named above; an argument that names none is the same for every part. Nothing has to cross between parts.
Inputs may be any that keep to these rules, and one draw needn't show every extreme that they name: For k < 12, neighbours[i,k] differs from i by 1 to 64. For k >= 12: in each aligned block of 64 rows, at most 33 of these entries fall into any one aligned block of 64 residues, and exactly 33 into some block.
All inputs are finite; a program needn't handle non-finite values.
Results may differ from a plain program's by a relative error of at most 0.014.
Values may be sent and summed in bfloat16 or wider, within the bound.
A program may use at most 64 MiB of HBM per device.

v0:
```python
import jax
import jax.numpy as jnp
from jax import lax
from jax.sharding import PartitionSpec as P

KL = 12


gelu_scale = 0.7978845608028654
gelu_cubic = 0.044715


def extended(cells, sides, width):
    for axis, dim in sides:
        count = lax.axis_size(axis)
        ends = count - 1
        head = lax.slice_in_dim(cells, 0, width, axis=dim)
        tail = lax.slice_in_dim(cells, cells.shape[dim] - width, cells.shape[dim], axis=dim)
        cells = jnp.concatenate(
            [
                lax.ppermute(tail, axis, [(i, (i + 1) % count) for i in range(ends)]),
                cells,
                lax.ppermute(head, axis, [((i + 1) % count, i) for i in range(ends)]),
            ],
            axis=dim,
        )
    return cells


def shifted(x, axis, by):
    count = lax.axis_size(axis)
    pairs = [(i, i + by) for i in range(count) if 0 <= i + by < count]
    return lax.ppermute(x, axis, pairs)


def gelu_parts(preact):
    inner = gelu_scale * (preact + gelu_cubic * preact * preact * preact)
    tangent = jnp.tanh(inner)
    values = 0.5 * preact * (1.0 + tangent)
    slopes = 0.5 * (1.0 + tangent) + 0.5 * preact * (1.0 - tangent * tangent) * gelu_scale * (
        1.0 + 3.0 * gelu_cubic * preact * preact
    )
    return (values, slopes)


def contract_rows(left, right):
    return lax.dot_general(
        left, right, (((0,), (0,)), ((), ())), preferred_element_type=jnp.float32
    )


def local(
    node_feats,
    edge_feats,
    neighbours,
    w_self,
    w_nbr,
    w_edge,
    bias,
    w_edge_out,
    w_node_out,
    grad_nodes,
    grad_edges,
):
    res_rows = node_feats.shape[0]
    nbr_count = neighbours.shape[1]
    long_count = nbr_count - KL
    node_width = node_feats.shape[1]
    edge_width = edge_feats.shape[2]
    hidden = w_self.shape[1]
    edges_dev = res_rows * nbr_count
    blocks_res = lax.axis_size("res")
    my_block = lax.axis_index("res")
    capacity = res_rows * long_count // blocks_res + 1
    total_slots = blocks_res * capacity
    padded = extended(node_feats, (("res", 0),), res_rows)
    local_index = (neighbours[:, :KL] - my_block * res_rows + res_rows).reshape(-1)
    window_rows = jnp.take(padded, local_index, axis=0).reshape(res_rows, KL, node_width)
    long_ids = neighbours[:, KL:].reshape(-1)
    owners = long_ids // res_rows
    onehot = (owners[:, None] == jnp.arange(blocks_res, dtype=jnp.int32)[None, :]).astype(jnp.int32)
    ranks = jnp.sum(onehot * jnp.cumsum(onehot, axis=0), axis=1) - 1
    slots = owners * capacity + ranks
    asked = (
        jnp.full((total_slots,), -1, jnp.int32)
        .at[slots]
        .set(long_ids % res_rows)
        .reshape(blocks_res, capacity)
    )
    wanted = lax.all_to_all(asked, "res", split_axis=0, concat_axis=0, tiled=True).reshape(-1)
    outgoing = jnp.take(node_feats, jnp.maximum(wanted, 0), axis=0).reshape(
        blocks_res, capacity, node_width
    )
    arrived = lax.all_to_all(outgoing, "res", split_axis=0, concat_axis=0, tiled=True).reshape(
        total_slots, node_width
    )
    long_rows = jnp.take(arrived, slots, axis=0)
    nbr_rows = jnp.concatenate(
        [window_rows, long_rows.reshape(res_rows, long_count, node_width)], axis=1
    ).reshape(edges_dev, node_width)
    edge_flat = edge_feats.reshape(edges_dev, edge_width)
    gedge_flat = grad_edges.reshape(edges_dev, edge_width)
    preact = jnp.dot(node_feats, w_self, preferred_element_type=jnp.float32)[:, None, :]
    preact = preact + jnp.dot(nbr_rows, w_nbr, preferred_element_type=jnp.float32).reshape(
        res_rows, nbr_count, hidden
    )
    preact = preact + jnp.dot(edge_flat, w_edge, preferred_element_type=jnp.float32).reshape(
        res_rows, nbr_count, hidden
    )
    preact = preact + bias
    values, slopes = gelu_parts(preact)
    message = values.astype(jnp.bfloat16)
    grad_msg = jnp.dot(gedge_flat, w_edge_out.T, preferred_element_type=jnp.float32).reshape(
        res_rows, nbr_count, hidden
    )
    grad_msg = (
        grad_msg
        + (jnp.dot(grad_nodes, w_node_out.T, preferred_element_type=jnp.float32) / nbr_count)[
            :, None, :
        ]
    )
    grad_pre = (grad_msg * slopes).astype(jnp.bfloat16)
    pre_flat = grad_pre.reshape(edges_dev, hidden)
    msg_flat = message.reshape(edges_dev, hidden)
    pre_sum = jnp.sum(grad_pre.astype(jnp.float32), axis=1).astype(jnp.bfloat16)
    msg_sum = jnp.sum(message.astype(jnp.float32), axis=1).astype(jnp.bfloat16)
    grads_local = (
        contract_rows(node_feats, pre_sum),
        contract_rows(nbr_rows, pre_flat),
        contract_rows(edge_flat, pre_flat),
        jnp.sum(pre_flat.astype(jnp.float32), axis=0),
        contract_rows(msg_flat, gedge_flat),
        contract_rows(msg_sum, grad_nodes) / nbr_count,
    )
    grad_self, grad_nbr, grad_edge_in, grad_bias, grad_eout, grad_nout = lax.psum(
        (
            grads_local[0],
            grads_local[1],
            grads_local[2],
            grads_local[3],
            grads_local[4],
            grads_local[5],
        ),
        "res",
    )
    feat_index = lax.axis_index("feat")
    feat_count = lax.axis_size("feat")
    edge_part = edge_width // feat_count
    node_part = node_width // feat_count
    full_pre, full_wedge = (
        lax.all_gather(pre_flat, "feat", axis=1, tiled=True),
        lax.all_gather(w_edge, "feat", axis=1, tiled=True),
    )
    own_wedge = lax.dynamic_slice_in_dim(full_wedge, feat_index * edge_part, edge_part, 0)
    edge_summed = jnp.dot(full_pre, own_wedge.T, preferred_element_type=jnp.float32)
    gedge_part = lax.dynamic_slice_in_dim(gedge_flat, feat_index * edge_part, edge_part, 1).astype(
        jnp.float32
    )
    d_edges = (
        (edge_summed + gedge_part).astype(jnp.bfloat16).reshape(res_rows, nbr_count, edge_part)
    )
    nbr_terms = jnp.dot(pre_flat, w_nbr.T, preferred_element_type=jnp.float32).reshape(
        res_rows, nbr_count, node_width
    )
    window_terms = nbr_terms[:, :KL, :].reshape(-1, node_width)
    long_terms = nbr_terms[:, KL:, :].reshape(-1, node_width)
    padded_grad = (
        jnp.zeros((3 * res_rows, node_width), jnp.float32).at[local_index].add(window_terms)
    )
    padded_grad = padded_grad.at[res_rows : 2 * res_rows].add(
        jnp.dot(pre_sum, w_self.T, preferred_element_type=jnp.float32)
    )
    slot_grad = jnp.zeros((total_slots, node_width), jnp.float32).at[slots].set(long_terms)
    node_terms = jnp.concatenate([padded_grad, slot_grad], axis=0)
    columns = node_terms.shape[1]
    from_below = shifted(
        node_terms[2 * res_rows : 3 * res_rows].astype(jnp.bfloat16), "res", 1
    ).astype(jnp.float32)
    from_above = shifted(node_terms[0:res_rows].astype(jnp.bfloat16), "res", -1).astype(jnp.float32)
    returned = lax.all_to_all(
        node_terms[3 * res_rows :].reshape(blocks_res, capacity, columns),
        "res",
        split_axis=0,
        concat_axis=0,
        tiled=True,
    ).reshape(total_slots, columns)
    node_total = node_terms[res_rows : 2 * res_rows] + from_below + from_above
    valid = (wanted >= 0)[:, None]
    node_total = node_total.at[jnp.maximum(wanted, 0)].add(jnp.where(valid, returned, 0.0))
    node_total = lax.psum_scatter(node_total, "feat", scatter_dimension=1, tiled=True)
    gnode_part = lax.dynamic_slice_in_dim(grad_nodes, feat_index * node_part, node_part, 1).astype(
        jnp.float32
    )
    d_nodes = (node_total + gnode_part).astype(jnp.bfloat16)
    return (
        d_nodes,
        d_edges,
        grad_self.astype(jnp.bfloat16),
        grad_nbr.astype(jnp.bfloat16),
        grad_edge_in.astype(jnp.bfloat16),
        grad_bias,
        grad_eout.astype(jnp.bfloat16),
        grad_nout.astype(jnp.bfloat16),
    )


def solution(mesh):
    in_specs = (
        P(("groups", "res"), None),
        P(("groups", "res"), None, None),
        P(("groups", "res"), None),
        P(None, "feat"),
        P(None, "feat"),
        P(None, "feat"),
        P("feat"),
        P("feat", None),
        P("feat", None),
        P(("groups", "res"), None),
        P(("groups", "res"), None, None),
    )
    out_specs = (
        P(("groups", "res"), "feat"),
        P(("groups", "res"), None, "feat"),
        P("groups", "feat"),
        P("groups", "feat"),
        P("groups", "feat"),
        P(("groups", "feat")),
        P(("groups", "feat"), None),
        P(("groups", "feat"), None),
    )
    return jax.shard_map(local, mesh=mesh, in_specs=in_specs, out_specs=out_specs, check_vma=False)
```

profile of v0, /device:TPU:0, one launch (start us, length us, event | category | flops | bytes accessed | tf_op | source)
XLA Modules:
  0.0 186.7 jit_solution(14199760694192457137)
XLA Ops:
  0.7 1.4 collective-permute-start.1
  2.1 3.0 %collective-permute-start = (bf16[64,512]{1,0:T(8,128)(2,1)}, bf16[64,512]{1,0:T(8,128)(2,1)S(1)}, u32[]{:S(2)}, u32[]{:S(2)}) collective-permute-start(bf16[64,512]{1,0:T(8,128)(2,1)} %param.13), channel_id=1, source_target_pairs={{0,1},{1,2},{2,3},{3,4},{4,5},{5,6},{6,7},{7,8},{8,9},{9,10},{10,1... | collective-permute-start | bytes 196616 | tf_op jit(solution)/shard_map/ppermute | solution.py:21
  5.1 0.7 slice.47
  6.2 1.2 reduce-window.6
  7.8 2.4 %scatter_custom_fusion = s32[528]{0:T(1024)S(1)} fusion(s32[512]{0:T(512)S(1)} %bitcast.80, s32[512]{0:T(512)S(1)} %get-tuple-element.72, s32[]{:T(128)} %constant.136.clone.1), kind=kCustom, calls=%fused_computation.98 | custom fusion | bytes 2116 | tf_op jit(solution)/shard_map/scatter | solution.py:87
  10.2 0.7 all_to_all.12
  10.9 7.9 %all-to-all-start = ((s32[16,1,33]{2,1,0:T(1,128)}), s32[16,1,33]{2,1,0:T(1,128)S(1)}, u32[]{:S(2)}, u32[]{:S(2)}) async-start(s32[16,1,33]{2,1,0:T(1,128)} %all_to_all.12), calls=%async_computation | async-start | bytes 16384 | tf_op jit(solution)/shard_map/all_to_all | solution.py:90
  18.9 0.7 compare_and_fusion
  19.6 0.7 fusion.27
  20.6 0.7 compare_and_fusion.1
  21.4 3.8 %all-to-all-done = s32[16,1,33]{2,1,0:T(1,128)S(1)} async-done(((s32[16,1,33]{2,1,0:T(1,128)}), s32[16,1,33]{2,1,0:T(1,128)S(1)}, u32[]{:S(2)}, u32[]{:S(2)}) %all-to-all-start) | async-done | bytes 2144 | tf_op jit(solution)/shard_map/all_to_all | solution.py:90
  25.3 2.7 %gather_fusion.1 = bf16[528,512]{1,0:T(8,128)(2,1)S(1)} fusion(bf16[64,512]{1,0:T(8,128)(2,1)S(1)} %copy-done.1, s32[1024]{0:T(1024)S(1)} %pad_clamp_fusion.1), kind=kCustom, calls=%fused_computation.1 | custom fusion | bytes 1083456 | tf_op jit(solution)/shard_map/jit(_take)/gather | solution.py:91
  28.2 1.0 broadcast_select_fusion
  29.2 3.8 %all-to-all-start.1 = ((bf16[16,33,512]{2,1,0:T(8,128)(2,1)}), bf16[16,33,512]{2,1,0:T(8,128)(2,1)S(1)}, u32[]{:S(2)}, u32[]{:S(2)}) async-start(bf16[16,33,512]{2,1,0:T(8,128)(2,1)} %broadcast_select_fusion), calls=%async_computation.1 | async-start | bytes 1310720 | tf_op jit(solution)/shard_map/all_to_all | solution.py:94
  33.0 1.5 copy.77
  34.5 1.2 reshape.329
  35.7 0.8 fusion.43
  36.5 1.2 convolution_multiply_fusion.1
  37.8 2.7 %gather_fusion = bf16[768,512]{1,0:T(8,128)(2,1)S(1)} fusion(bf16[192,512]{1,0:T(8,128)(2,1)S(1)} %pad_maximum_fusion.3, s32[1024]{0:T(1024)S(1)} %pad_clamp_fusion.2), kind=kCustom, calls=%fused_computation | custom fusion | bytes 1575936 | tf_op jit(solution)/shard_map/jit(_take)/gather | solution.py:78
  40.7 1.8 copy_select_fusion
  42.6 6.8 %all-to-all-done.1 = bf16[16,33,512]{2,1,0:T(8,128)(2,1)S(1)} async-done(((bf16[16,33,512]{2,1,0:T(8,128)(2,1)}), bf16[16,33,512]{2,1,0:T(8,128)(2,1)S(1)}, u32[]{:S(2)}, u32[]{:S(2)}) %all-to-all-start.1) | async-done | bytes 540704 | tf_op jit(solution)/shard_map/all_to_all | solution.py:94
  49.6 2.0 %gather_fusion.2 = bf16[512,512]{1,0:T(8,128)(2,1)S(1)} fusion(bf16[528,512]{1,0:T(8,128)(2,1)S(1)} %reshape.322, s32[1024]{0:T(1024)S(1)} %pad_clamp_fusion), kind=kCustom, calls=%fused_computation.2 | custom fusion | bytes 1050624 | tf_op jit(solution)/shard_map/jit(_take)/gather | solution.py:97
  52.9 0.7 fusion.40
  54.0 1.1 fusion.42
  55.1 1.3 copy.76
  56.9 1.5 copy-done.2
  58.4 1.1 convolution_bitcast_fusion.2
  59.6 3.1 %scatter_custom_fusion.2 = f32[528,512]{1,0:T(8,128)S(1)} fusion(s32[512]{0:T(512)S(1)} %bitcast.82, f32[64,8,512]{2,0,1:T(8,128)S(1)} %slice-done, f32[]{:T(128)} %constant.124.clone.1), kind=kCustom, calls=%fused_computation.34 | custom fusion | bytes 2129924 | tf_op jit(solution)/shard_map/scatter | solution.py:173
  62.7 1.2 reshape.325
  64.0 4.9 %all-to-all-start.2 = ((f32[16,33,512]{2,1,0:T(8,128)}), f32[16,33,512]{2,1,0:T(8,128)}, u32[]{:S(2)}, u32[]{:S(2)}) async-start(f32[16,33,512]{2,1,0:T(8,128)} %reshape.325), calls=%async_computation.2 | async-start | bytes 2621440 | tf_op jit(solution)/shard_map/all_to_all | solution.py:180
  68.9 1.1 convolution_multiply_fusion
  70.0 1.4 convolution_bitcast_fusion
  71.4 1.1 convolution_bitcast_fusion.3
  72.4 1.1 convolution_bitcast_fusion.1
  73.5 2.0 %reshape.327 = bf16[1280,256]{1,0:T(8,128)(2,1)} reshape(bf16[64,20,256]{2,1,0:T(8,128)(2,1)} %copy.76) | data formatting | bytes 1310720 | tf_op jit(solution)/shard_map/reshape | solution.py:123
  75.5 2.3 %copy.73 = f32[64,12,512]{2,1,0:T(8,128)} copy(f32[64,12,512]{2,0,1:T(8,128)S(1)} %slice-done.1) | data formatting | bytes 3145728 | tf_op jit(solution)/shard_map/slice | solution.py:165
  77.8 2.5 %reshape.366 = f32[768,512]{1,0:T(8,128)} reshape(f32[64,12,512]{2,1,0:T(8,128)} %copy.73) | data formatting | bytes 3145728 | tf_op jit(solution)/shard_map/reshape | solution.py:165
  80.3 7.4 %scatter_custom_fusion.1 = f32[192,512]{1,0:T(8,128)S(1)} fusion(s32[768]{0:T(1024)S(1)} %fusion.32, f32[768,512]{1,0:T(8,128)} %reshape.366, f32[]{:T(128)} %constant.124.clone.1), kind=kCustom, calls=%fused_computation.47 | custom fusion | flops 393216 | bytes 393728 | tf_op jit(solution)/shard_map/scatter-add | solution.py:168
  88.5 2.2 %collective-permute-start.2 = (bf16[64,512]{1,0:T(8,128)(2,1)}, bf16[64,512]{1,0:T(8,128)(2,1)S(1)}, u32[]{:S(2)}, u32[]{:S(2)}) collective-permute-start(bf16[64,512]{1,0:T(8,128)(2,1)} %get-tuple-element.68), channel_id=1, source_target_pairs={{0,1},{1,2},{2,3},{3,4},{4,5},{5,6},{6,7},{7,8},{8,9},{9,10},{10,1... | collective-permute-start | bytes 196616 | tf_op jit(solution)/shard_map/ppermute | solution.py:33
  90.7 1.3 collective-permute-start.3
  92.2 1.4 fusion
  93.7 78.3 %all-reduce.2 = (bf16[512,256]{0,1:T(8,128)(2,1)S(1)}, bf16[512,256]{1,0:T(8,128)(2,1)}, bf16[256,256]{0,1:T(8,128)(2,1)S(1)}, f32[256]{0:T(256)}, bf16[256,256]{1,0:T(8,128)(2,1)}, /*index=5*/bf16[256,512]{1,0:T(8,128)(2,1)}) all-reduce(f32[512,256]{0,1:T(8,128)} %convolution_bitcast_fusion.1, ...), channel_id=1, replica_groups=mesh['groups'=2,'res'=16,'feat'=1] {'res'}, use_global_device_ids=true, to_apply=%region_8.9 | all-reduce | flops 524544 | bytes 3147776 | tf_op jit(solution)/shard_map/psum | solution.py:135
  172.0 0.8 copy.79
  172.8 0.8 copy.80
  173.7 1.0 copy.78
  174.7 1.1 convert_add_fusion
  175.8 1.5 reshape.326
  177.3 8.8 %scatter_custom_fusion.3 = f32[64,512]{1,0:T(8,128)S(1)} fusion(f32[64,512]{1,0:T(8,128)S(1)} %convert_add_fusion, s32[528]{0:T(1024)S(1)} %reshape.340, f32[528,512]{1,0:T(8,128)S(1)} %reshape.326, f32[]{:T(128)} %constant.124.clone.1, pred[528]{0:T(1024)(128)(4,1)S(1)} %ge.40), kind=kCustom, calls=%fused_computation.32 | custom fusion | flops 540672 | bytes 1213444 | tf_op jit(solution)/shard_map/scatter-add | solution.py:189
  (87 shorter events, 5.9 us)
Async XLA Ops:
  0.6 52.0 %copy-start = (bf16[64,20,256]{2,0,1:T(8,128)(2,1)S(1)}, bf16[64,20,256]{2,0,1:T(8,128)(2,1)}, u32[]{:S(2)}) copy-start(bf16[64,20,256]{2,0,1:T(8,128)(2,1)} %param.14) | copy-start | bytes 1966084
  0.6 24.7 %copy-start.1 = (bf16[64,512]{1,0:T(8,128)(2,1)S(1)}, bf16[64,512]{1,0:T(8,128)(2,1)}, u32[]{:S(2)}) copy-start(bf16[64,512]{1,0:T(8,128)(2,1)} %param.13) | copy-start | bytes 196612
  0.7 37.1 %collective-permute-start.1 = (bf16[64,512]{1,0:T(8,128)(2,1)}, bf16[64,512]{1,0:T(8,128)(2,1)S(1)}, u32[]{:S(2)}, u32[]{:S(2)}) collective-permute-start(bf16[64,512]{1,0:T(8,128)(2,1)} %param.13), channel_id=1, source_target_pairs={{1,0},{2,1},{3,2},{4,3},{5,4},{6,5},{7,6},{8,7},{9,8},{10,9},{11,1... | collective-permute-start | bytes 196616 | tf_op jit(solution)/shard_map/ppermute | solution.py:23
  2.1 35.7 %collective-permute-start = (bf16[64,512]{1,0:T(8,128)(2,1)}, bf16[64,512]{1,0:T(8,128)(2,1)S(1)}, u32[]{:S(2)}, u32[]{:S(2)}) collective-permute-start(bf16[64,512]{1,0:T(8,128)(2,1)} %param.13), channel_id=1, source_target_pairs={{0,1},{1,2},{2,3},{3,4},{4,5},{5,6},{6,7},{7,8},{8,9},{9,10},{10,1... | collective-permute-start | bytes 196616 | tf_op jit(solution)/shard_map/ppermute | solution.py:21
  10.9 14.3 %all-to-all-start = ((s32[16,1,33]{2,1,0:T(1,128)}), s32[16,1,33]{2,1,0:T(1,128)S(1)}, u32[]{:S(2)}, u32[]{:S(2)}) async-start(s32[16,1,33]{2,1,0:T(1,128)} %all_to_all.12), calls=%async_computation | async-start | bytes 16384 | tf_op jit(solution)/shard_map/all_to_all | solution.py:90
  29.2 20.2 %all-to-all-start.1 = ((bf16[16,33,512]{2,1,0:T(8,128)(2,1)}), bf16[16,33,512]{2,1,0:T(8,128)(2,1)S(1)}, u32[]{:S(2)}, u32[]{:S(2)}) async-start(bf16[16,33,512]{2,1,0:T(8,128)(2,1)} %broadcast_select_fusion), calls=%async_computation.1 | async-start | bytes 1310720 | tf_op jit(solution)/shard_map/all_to_all | solution.py:94
  34.5 1.2 copy-start.6
  34.5 2.0 %copy-start.11 = (bf16[64,512]{1,0:T(8,128)(2,1)S(1)}, bf16[64,512]{1,0:T(8,128)(2,1)}, u32[]{:S(2)}) copy-start(bf16[64,512]{1,0:T(8,128)(2,1)} %param.22) | copy-start | bytes 196612
  49.6 2.2 %copy-start.8 = (bf16[64,12,512]{2,0,1:T(8,128)(2,1)S(1)}, bf16[64,12,512]{2,0,1:T(8,128)(2,1)}, u32[]{:S(2)}) copy-start(bf16[64,12,512]{2,0,1:T(8,128)(2,1)} %copy_select_fusion) | copy-start | bytes 2359300
  49.6 2.2 %copy-start.14 = (bf16[512,256]{1,0:T(8,128)(2,1)S(1)}, bf16[512,256]{1,0:T(8,128)(2,1)}, u32[]{:S(2)}) copy-start(bf16[512,256]{1,0:T(8,128)(2,1)} %param.17) | copy-start | bytes 786436
  49.6 2.2 %copy-start.18 = (f32[64,256]{1,0:T(8,128)S(1)}, f32[64,256]{1,0:T(8,128)}, u32[]{:S(2)}) copy-start(f32[64,256]{1,0:T(8,128)} %fusion.43) | copy-start | bytes 196612
  51.8 0.8 copy-start.12
  51.8 1.0 copy-start.16
  51.8 1.0 copy-start.20
  52.9 1.1 copy-start.10
  52.9 1.1 copy-start.19
  55.0 1.8 copy-start.3
  55.1 1.3 copy-start.15
  56.9 1.5 copy-start.2
  58.4 1.2 slice-start
  64.0 6.0 %copy-start.4 = (bf16[64,20,256]{2,0,1:T(8,128)(2,1)S(1)}, bf16[64,20,256]{2,0,1:T(8,128)(2,1)}, u32[]{:S(2)}) copy-start(bf16[64,20,256]{2,0,1:T(8,128)(2,1)} %copy-done.3) | copy-start | bytes 1966084
  64.0 6.0 %copy-start.9 = (bf16[64,12,512]{2,0,1:T(8,128)(2,1)S(1)}, bf16[64,12,512]{2,0,1:T(8,128)(2,1)}, u32[]{:S(2)}) copy-start(bf16[64,12,512]{2,0,1:T(8,128)(2,1)} %copy_select_fusion) | copy-start | bytes 2359300
  64.0 6.0 %copy-start.13 = (bf16[64,8,512]{2,0,1:T(8,128)(2,1)S(1)}, bf16[64,8,512]{2,0,1:T(8,128)(2,1)}, u32[]{:S(2)}) copy-start(bf16[64,8,512]{2,0,1:T(8,128)(2,1)} %copy-done.12) | copy-start | bytes 1572868
  64.0 111.8 %all-to-all-start.2 = ((f32[16,33,512]{2,1,0:T(8,128)}), f32[16,33,512]{2,1,0:T(8,128)}, u32[]{:S(2)}, u32[]{:S(2)}) async-start(f32[16,33,512]{2,1,0:T(8,128)} %reshape.325), calls=%async_computation.2 | async-start | bytes 2621440 | tf_op jit(solution)/shard_map/all_to_all | solution.py:180
  72.4 3.1 %slice-start.1 = ((f32[64,20,512]{2,0,1:T(8,128)}), f32[64,12,512]{2,0,1:T(8,128)S(1)}, s32[]{:S(2)}) async-start(f32[64,20,512]{2,0,1:T(8,128)} %copy-done.2), calls=%async_computation.4 | async-start | bytes 3145728 | tf_op jit(solution)/shard_map/slice | solution.py:165
  80.3 11.9 %copy-start.5 = (f32[1280,256]{1,0:T(8,128)S(1)}, f32[1280,256]{1,0:T(8,128)}, u32[]{:S(2)}) copy-start(f32[1280,256]{1,0:T(8,128)} %reshape.329) | copy-start | bytes 3932164
  87.8 4.4 %copy-start.17 = (bf16[256,256]{1,0:T(8,128)(2,1)S(1)}, bf16[256,256]{1,0:T(8,128)(2,1)}, u32[]{:S(2)}) copy-start(bf16[256,256]{1,0:T(8,128)(2,1)} %param.18) | copy-start | bytes 393220
  88.5 86.2 %collective-permute-start.2 = (bf16[64,512]{1,0:T(8,128)(2,1)}, bf16[64,512]{1,0:T(8,128)(2,1)S(1)}, u32[]{:S(2)}, u32[]{:S(2)}) collective-permute-start(bf16[64,512]{1,0:T(8,128)(2,1)} %get-tuple-element.68), channel_id=1, source_target_pairs={{0,1},{1,2},{2,3},{3,4},{4,5},{5,6},{6,7},{7,8},{8,9},{9,10},{10,1... | collective-permute-start | bytes 196616 | tf_op jit(solution)/shard_map/ppermute | solution.py:33
  90.7 84.0 %collective-permute-start.3 = (bf16[64,512]{1,0:T(8,128)(2,1)}, bf16[64,512]{1,0:T(8,128)(2,1)}, u32[]{:S(2)}, u32[]{:S(2)}) collective-permute-start(bf16[64,512]{1,0:T(8,128)(2,1)} %get-tuple-element.69), channel_id=1, source_target_pairs={{1,0},{2,1},{3,2},{4,3},{5,4},{6,5},{7,6},{8,7},{9,8},{10,9},{11,1... | collective-permute-start | bytes 196616 | tf_op jit(solution)/shard_map/ppermute | solution.py:33
  173.6 1.1 copy-start.7
where the time goes:
time: 188 us; the launch traced here: 187 us
  blocking collectives  78.3 us (42%)
  local copies, waits for them, and re-layouts  35.4 us (19%)
  starting transfers between devices  24.6 us (13%)
  other arithmetic  23.6 us (13%)
  matrix products  12.9 us (7%)
  waiting for transfers between devices  10.7 us (6%)
    psum x1, blocking collectives, local(): lax.psum((grads_local[0], grads_local[1], grads_local[2], grads_local[3],...  78.3 us
    scatter-add x1, other arithmetic, local(): node_total.at[jnp.maximum(wanted, 0)].add(jnp.where(valid, returned, 0.0))  8.79 us
    all_to_all x1, starting transfers between devices, local(): lax.all_to_all(asked, 'res', split_axis=0, concat_axis=0, tiled=True)  7.92 us
    scatter-add x1, other arithmetic, local(): jnp.zeros((3 * res_rows, node_width), jnp.float32).at[local_index]  7.44 us
    all_to_all x1, waiting for transfers between devices, local(): lax.all_to_all(outgoing, 'res', split_axis=0, concat_axis=0, tiled=True)  6.83 us
    dot_general x5, matrix products, contract_rows(): lax.dot_general(left, right, (((0,), (0,)), ((), ())), preferred_element_...  5.69 us
    unnamed x45, local copies, waits for them, and re-layouts  5.06 us
    all_to_all x1, starting transfers between devices, local(): lax.all_to_all(node_terms[3 * res_rows:].reshape(blocks_res, capacity, co...  4.9 us
  transfers between devices with their start and end apart: 7, of which 2 were waited for; matrix products, arithmetic and copies ran while one was open for 25% of the time, Pallas kernels for 0%

commit v1 on v0

v1 whole, which is shorter than its diff:
```python
import jax
import jax.numpy as jnp
from jax import lax
from jax.sharding import PartitionSpec as P

gelu_scale = 0.7978845608028654
gelu_cubic = 0.044715


def gelu_parts(preact):
    inner = gelu_scale * (preact + gelu_cubic * preact * preact * preact)
    tangent = jnp.tanh(inner)
    values = 0.5 * preact * (1.0 + tangent)
    slopes = 0.5 * (1.0 + tangent) + 0.5 * preact * (1.0 - tangent * tangent) * gelu_scale * (
        1.0 + 3.0 * gelu_cubic * preact * preact
    )
    return (values, slopes)


def contract_rows(left, right):
    return lax.dot_general(
        left, right, (((0,), (0,)), ((), ())), preferred_element_type=jnp.float32
    )


def local(
    node_feats,
    edge_feats,
    neighbours,
    w_self,
    w_nbr,
    w_edge,
    bias,
    w_edge_out,
    w_node_out,
    grad_nodes,
    grad_edges,
):
    res_rows = node_feats.shape[0]
    nbr_count = neighbours.shape[1]
    node_width = node_feats.shape[1]
    edge_width = edge_feats.shape[2]
    hidden = w_self.shape[1]
    edges_dev = res_rows * nbr_count
    blocks_res = lax.axis_size("res")
    nodes_all = res_rows * blocks_res
    edge_flat = edge_feats.reshape(edges_dev, edge_width)
    gedge_flat = grad_edges.reshape(edges_dev, edge_width)
    projected = jnp.dot(node_feats, w_nbr, preferred_element_type=jnp.float32).astype(jnp.bfloat16)
    table = lax.all_gather(projected, "res", axis=0, tiled=True)
    picks = (
        neighbours.reshape(-1)[:, None] == jnp.arange(nodes_all, dtype=jnp.int32)[None, :]
    ).astype(jnp.bfloat16)
    preact = (jnp.dot(node_feats, w_self, preferred_element_type=jnp.float32) + bias)[:, None, :]
    preact = preact + (
        jnp.dot(edge_flat, w_edge, preferred_element_type=jnp.float32)
        + jnp.dot(picks, table, preferred_element_type=jnp.float32)
    ).reshape(res_rows, nbr_count, hidden)
    values, slopes = gelu_parts(preact)
    message = values.astype(jnp.bfloat16)
    grad_msg = jnp.dot(gedge_flat, w_edge_out.T, preferred_element_type=jnp.float32).reshape(
        res_rows, nbr_count, hidden
    )
    grad_msg = (
        grad_msg
        + (jnp.dot(grad_nodes, w_node_out.T, preferred_element_type=jnp.float32) / nbr_count)[
            :, None, :
        ]
    )
    grad_pre = (grad_msg * slopes).astype(jnp.bfloat16)
    pre_flat = grad_pre.reshape(edges_dev, hidden)
    msg_flat = message.reshape(edges_dev, hidden)
    pre_sum = jnp.sum(grad_pre.astype(jnp.float32), axis=1).astype(jnp.bfloat16)
    msg_sum = jnp.sum(message.astype(jnp.float32), axis=1).astype(jnp.bfloat16)
    spread = contract_rows(picks, pre_flat).astype(jnp.bfloat16)
    landed = lax.all_to_all(
        spread.reshape(blocks_res, res_rows, hidden), "res", split_axis=0, concat_axis=0, tiled=True
    )
    reached = jnp.sum(landed.astype(jnp.float32), axis=0).astype(jnp.bfloat16)
    terms = (
        contract_rows(node_feats, pre_sum),
        contract_rows(node_feats, reached),
        contract_rows(edge_flat, pre_flat),
        contract_rows(msg_flat, gedge_flat),
        contract_rows(msg_sum, grad_nodes) / nbr_count,
    )
    packed = jnp.concatenate(
        [t.astype(jnp.bfloat16).reshape(blocks_res, -1, 128) for t in terms], axis=1
    )
    swapped = lax.all_to_all(packed, "res", split_axis=0, concat_axis=0, tiled=True)
    mine = jnp.sum(swapped.astype(jnp.float32), axis=0).astype(jnp.bfloat16)
    totals = lax.all_gather(mine, "res", axis=0, tiled=False)
    outs = []
    start = 0
    for t in terms:
        rows = t.size // blocks_res // 128
        outs.append(totals[:, start : start + rows].reshape(t.shape))
        start += rows
    grad_self, grad_nbr, grad_edge_in, grad_eout, grad_nout = outs
    grad_bias = lax.psum(jnp.sum(pre_flat.astype(jnp.float32), axis=0), "res")
    feat_index = lax.axis_index("feat")
    feat_count = lax.axis_size("feat")
    edge_part = edge_width // feat_count
    node_part = node_width // feat_count
    full_pre, full_wedge = (
        lax.all_gather(pre_flat, "feat", axis=1, tiled=True),
        lax.all_gather(w_edge, "feat", axis=1, tiled=True),
    )
    own_wedge = lax.dynamic_slice_in_dim(full_wedge, feat_index * edge_part, edge_part, 0)
    edge_summed = jnp.dot(full_pre, own_wedge.T, preferred_element_type=jnp.float32)
    gedge_part = lax.dynamic_slice_in_dim(gedge_flat, feat_index * edge_part, edge_part, 1).astype(
        jnp.float32
    )
    d_edges = (
        (edge_summed + gedge_part).astype(jnp.bfloat16).reshape(res_rows, nbr_count, edge_part)
    )
    node_total = jnp.dot(pre_sum, w_self.T, preferred_element_type=jnp.float32) + jnp.dot(
        reached, w_nbr.T, preferred_element_type=jnp.float32
    )
    node_total = lax.psum_scatter(node_total, "feat", scatter_dimension=1, tiled=True)
    gnode_part = lax.dynamic_slice_in_dim(grad_nodes, feat_index * node_part, node_part, 1).astype(
        jnp.float32
    )
    d_nodes = (node_total + gnode_part).astype(jnp.bfloat16)
    return (d_nodes, d_edges, grad_self, grad_nbr, grad_edge_in, grad_bias, grad_eout, grad_nout)


def solution(mesh):
    in_specs = (
        P(("groups", "res"), None),
        P(("groups", "res"), None, None),
        P(("groups", "res"), None),
        P(None, "feat"),
        P(None, "feat"),
        P(None, "feat"),
        P("feat"),
        P("feat", None),
        P("feat", None),
        P(("groups", "res"), None),
        P(("groups", "res"), None, None),
    )
    out_specs = (
        P(("groups", "res"), "feat"),
        P(("groups", "res"), None, "feat"),
        P("groups", "feat"),
        P("groups", "feat"),
        P("groups", "feat"),
        P(("groups", "feat")),
        P(("groups", "feat"), None),
        P(("groups", "feat"), None),
    )
    return jax.shard_map(local, mesh=mesh, in_specs=in_specs, out_specs=out_specs, check_vma=False)
```

time: 188 us -> 148 us (0.79)
  other arithmetic: 23.6 us -> 1.68 us
  starting transfers between devices: 24.6 us -> 3.61 us
  local copies, waits for them, and re-layouts: 35.4 us -> 16.2 us
  between operations: 1.14 us -> 14.5 us
  blocking collectives: 78.3 us -> 86.9 us
    psum x1, blocking collectives: 78.3 us -> 33.7 us  [local(): grad_bias = lax.psum(jnp.sum(pre_flat.astype(jnp.float32), axis=0), 'res')]
    all_to_all x0 -> x1, blocking collectives: none -> 28.7 us  [local(): lax.all_to_all(packed, 'res', split_axis=0, concat_axis=0, tiled=True)]
    all_gather x0 -> x1, blocking collectives: none -> 24.6 us  [local(): table = lax.all_gather(projected, 'res', axis=0, tiled=True)]
    scatter-add x2 -> x0, other arithmetic: 16.2 us -> none  [the longest x1 8.79 us: local(): node_total.at[jnp.maximum(wanted, 0)].add(jnp.where(valid, returned, 0.0))]
    all_to_all x3 -> x1, starting transfers between devices: 16.6 us -> 3.57 us  [local(): lax.all_to_all(spread.reshape(blocks_res, res_rows, hidden), 'res', split...]
    ppermute x4 -> x0, starting transfers between devices: 7.99 us -> none  [the longest x2 3.54 us: shifted(): return lax.ppermute(x, axis, pairs)]
    gather x5 -> x0, local copies, waits for them, and re-layouts: 7.72 us -> none  [the longest x2 2.9 us: local(): jnp.take(node_feats, jnp.maximum(wanted, 0), axis=0)]
    scatter x2 -> x0, local copies, waits for them, and re-layouts: 5.56 us -> none  [the longest x1 3.12 us: local(): jnp.zeros((total_slots, node_width), jnp.float32).at[slots].set(long_terms)]
  transfers between devices with their start and end apart: 7 -> 2, of which waited for: 2 -> 1; matrix products, arithmetic and copies ran while one was open for 25% -> 6% of each run, Pallas kernels for 0% -> 0%
where the time goes in v1:
time: 148 us; the launch traced here: 147 us
  blocking collectives  86.9 us (59%)
  local copies, waits for them, and re-layouts  16.2 us (11%)
  between operations  14.5 us (10%)
  matrix products  13.7 us (9%)
  waiting for transfers between devices  10.7 us (7%)
  starting transfers between devices  3.61 us (2%)
  other arithmetic  1.68 us (1%)
    psum x1, blocking collectives, local(): grad_bias = lax.psum(jnp.sum(pre_flat.astype(jnp.float32), axis=0), 'res')  33.7 us
    all_to_all x1, blocking collectives, local(): lax.all_to_all(packed, 'res', split_axis=0, concat_axis=0, tiled=True)  28.7 us
    all_gather x1, blocking collectives, local(): table = lax.all_gather(projected, 'res', axis=0, tiled=True)  24.6 us
    all_to_all x1, waiting for transfers between devices, local(): lax.all_to_all(spread.reshape(blocks_res, res_rows, hidden), 'res', split...  10.7 us
    unnamed x47, local copies, waits for them, and re-layouts  5.8 us
    dot_general x6, matrix products, contract_rows(): lax.dot_general(left, right, (((0,), (0,)), ((), ())), preferred_element_...  5.14 us
    reshape x5, local copies, waits for them, and re-layouts, local(): outs.append(totals[:, start:start + rows].reshape(t.shape))  3.85 us
    all_to_all x1, starting transfers between devices, local(): lax.all_to_all(spread.reshape(blocks_res, res_rows, hidden), 'res', split...  3.57 us
  transfers between devices with their start and end apart: 2, of which 1 were waited for; matrix products, arithmetic and copies ran while one was open for 6% of the time, Pallas kernels for 0%

profile of v1, /device:TPU:0, one launch (start us, length us, event | category | flops | bytes accessed | tf_op | source)
XLA Modules:
  0.0 147.2 jit_solution(794926285674351523)
XLA Ops:
  7.2 0.9 copy.22
  8.2 1.2 convolution_convert_fusion.2
  9.3 24.6 %all_gather.11 = bf16[1024,256]{1,0:T(8,128)(2,1)S(1)} all-gather(bf16[64,256]{1,0:T(8,128)(2,1)S(1)} %convolution_convert_fusion.2), channel_id=1, replica_groups=mesh['groups'=2,'res'=16,'feat'=1] {'res'}, dimensions={0}, use_global_device_ids=true | all-gather | bytes 557056 | tf_op jit(solution)/shard_map/all_gather | solution.py:50
  33.9 0.4 copy.21
  34.4 1.1 fusion.1
  35.5 0.3 convolution_add_fusion.1
  35.9 0.1 reshape.73
  36.1 0.6 copy-done.4
  36.7 0.2 convolution_add_fusion.4
  36.9 0.2 convolution_multiply_fusion.1
  37.1 2.3 %fusion.25 = (bf16[64,256]{1,0:T(8,128)(2,1)S(1)}, bf16[64,20,256]{2,0,1:T(8,128)(2,1)S(1)}) fusion(f32[64,20,256]{2,1,0:T(8,128)S(1)} %reshape.73, f32[64,256]{1,0:T(8,128)S(1)} %convolution_add_fusion.4, f32[64,256]{1,0:T(8,128)S(1)} %convolution_multiply_fusion.1, bf16[64,20,256]{2,0,1:T(8,128)(2,1)} %param.21, bf16[256,256]{1,0:T(8,128)(2,1)} %param.18), kind=kOutput, calls=%fused_computation.48 | convolution fusion | flops 174964736 | bytes 2916352 | tf_op jit(solution)/shard_map/dot_general | solution.py:61
  39.5 0.4 copy.24
  39.8 1.0 reshape.74
  40.8 3.6 %fusion.12 = bf16[1024,256]{1,0:T(8,128)(2,1)} fusion(bf16[1280,256]{1,0:T(8,128)(2,1)} %reshape.74, s32[1280]{0:T(1024)S(1)} %eq.15), kind=kOutput, calls=%fused_computation.21 | convolution fusion | flops 672661504 | bytes 1184768 | tf_op jit(solution)/shard_map/dot_general | solution.py:21
  44.5 3.6 %all-to-all-start = ((bf16[16,64,256]{2,1,0:T(8,128)(2,1)}), bf16[16,64,256]{2,1,0:T(8,128)(2,1)S(1)}, u32[]{:S(2)}, u32[]{:S(2)}) async-start(bf16[16,64,256]{2,1,0:T(8,128)(2,1)} %bitcast.52), calls=%async_computation | async-start | bytes 1048576 | tf_op jit(solution)/shard_map/all_to_all | solution.py:76
  48.1 0.6 fusion.22
  48.7 0.4 copy-done.7
  49.2 0.4 fusion.17
  49.6 0.6 copy-done.6
  50.3 0.4 fusion.18
  50.8 0.2 fusion.14
  51.1 0.1 copy.26
  51.3 0.2 fusion.13
  51.6 0.2 reshape.81
  51.8 10.7 %all-to-all-done = bf16[16,64,256]{2,1,0:T(8,128)(2,1)S(1)} async-done(((bf16[16,64,256]{2,1,0:T(8,128)(2,1)}), bf16[16,64,256]{2,1,0:T(8,128)(2,1)S(1)}, u32[]{:S(2)}, u32[]{:S(2)}) %all-to-all-start) | async-done | bytes 524320 | tf_op jit(solution)/shard_map/all_to_all | solution.py:76
  62.5 0.6 copy-done.12
  63.2 0.2 fusion.15
  63.4 0.1 copy.27
  63.8 28.7 %all_to_all.10 = bf16[16,256,128]{2,1,0:T(8,128)(2,1)S(1)} all-to-all(bf16[16,256,128]{2,1,0:T(8,128)(2,1)S(1)} %constant_dynamic-update-slice_fusion), channel_id=1, replica_groups=mesh['groups'=2,'res'=16,'feat'=1] {'res'}, dimensions={0} | all-to-all | bytes 2097152 | tf_op jit(solution)/shard_map/all_to_all | solution.py:90
  92.5 0.8 reduce_sum.60
  93.3 0.3 copy-done.8
  93.6 0.4 copy.25
  94.0 0.1 reshape.87
  94.1 0.8 copy-done.11
  94.9 2.3 %fusion.4 = bf16[1280,256]{1,0:T(8,128)(2,1)} fusion(f32[1280,256]{1,0:T(8,128)S(1)} %reshape.87, bf16[1280,256]{1,0:T(8,128)(2,1)} %reshape.74, bf16[256,256]{1,0:T(8,128)(2,1)S(1)} %copy-done.11), kind=kOutput, calls=%fused_computation.7 | convolution fusion | flops 168427520 | bytes 2752512 | tf_op jit(solution)/shard_map/dot_general | solution.py:110
  97.2 1.3 reshape.76
  98.5 1.0 copy.29
  99.5 0.2 convert_reduce_fusion
  99.7 33.7 %psum.7 = f32[256]{0:T(256)} all-reduce(f32[256]{0:T(256)S(1)} %convert_reduce_fusion), channel_id=1, replica_groups=mesh['groups'=2,'res'=16,'feat'=1] {'res'}, use_global_device_ids=true, to_apply=%region_5.0 | all-reduce | flops 256 | bytes 2048 | tf_op jit(solution)/shard_map/psum | solution.py:100
  133.3 0.2 fusion.26
  133.5 0.8 fusion.20
  134.4 1.0 fusion.24
  135.4 1.2 fusion.23
  136.5 0.9 reshape.86
  137.4 0.7 reshape.85
  138.1 0.7 reshape.84
  138.8 0.8 reshape.83
  139.6 0.8 reshape.82
  (50 shorter events, 1.0 us)
Async XLA Ops:
  7.2 28.9 %copy-start = (bf16[512,256]{1,0:T(8,128)(2,1)S(1)}, bf16[512,256]{1,0:T(8,128)(2,1)}, u32[]{:S(2)}) copy-start(bf16[512,256]{1,0:T(8,128)(2,1)} %param.14) | copy-start | bytes 786436
  7.2 26.7 %copy-start.5 = (bf16[64,20,256]{2,0,1:T(8,128)(2,1)S(1)}, bf16[64,20,256]{2,0,1:T(8,128)(2,1)}, u32[]{:S(2)}) copy-start(bf16[64,20,256]{2,0,1:T(8,128)(2,1)} %param.12) | copy-start | bytes 1966084
  34.4 1.1 copy-start.10
  35.9 0.8 copy-start.4
  35.9 0.8 copy-start.19
  35.9 1.0 copy-start.9
  35.9 1.0 copy-start.14
  36.9 2.5 %copy-start.15 = (f32[64,256]{1,0:T(8,128)}, f32[64,256]{1,0:T(8,128)S(1)}, u32[]{:S(2)}) copy-start(f32[64,256]{1,0:T(8,128)S(1)} %convolution_add_fusion.4) | copy-start | bytes 196612
  39.5 10.2 %copy-start.1 = (bf16[64,20,256]{2,0,1:T(8,128)(2,1)}, bf16[64,20,256]{2,0,1:T(8,128)(2,1)S(1)}, u32[]{:S(2)}) copy-start(bf16[64,20,256]{2,0,1:T(8,128)(2,1)S(1)} %get-tuple-element.32) | copy-start | bytes 1966084
  39.5 11.4 %copy-start.17 = (bf16[64,256]{1,0:T(8,128)(2,1)}, bf16[64,256]{1,0:T(8,128)(2,1)S(1)}, u32[]{:S(2)}) copy-start(bf16[64,256]{1,0:T(8,128)(2,1)S(1)} %get-tuple-element.31) | copy-start | bytes 98308
  40.8 7.3 %copy-start.16 = (f32[64,256]{1,0:T(8,128)S(1)}, f32[64,256]{1,0:T(8,128)}, u32[]{:S(2)}) copy-start(f32[64,256]{1,0:T(8,128)} %copy-done.15) | copy-start | bytes 196612
  44.5 18.0 %all-to-all-start = ((bf16[16,64,256]{2,1,0:T(8,128)(2,1)}), bf16[16,64,256]{2,1,0:T(8,128)(2,1)S(1)}, u32[]{:S(2)}, u32[]{:S(2)}) async-start(bf16[16,64,256]{2,1,0:T(8,128)(2,1)} %bitcast.52), calls=%async_computation | async-start | bytes 1048576 | tf_op jit(solution)/shard_map/all_to_all | solution.py:76
  48.0 86.3 %all-gather.3.cloned.1.call-start = ((), (), s32[]{:S(2)}) async-start(), calls=%async_computation.2 | async-start | bytes 1114112 | tf_op jit(solution)/shard_map/all_gather | solution.py:92
  48.1 1.1 copy-start.7
  49.2 1.1 copy-start.6
  62.5 0.6 copy-start.12
  92.5 1.1 copy-start.8
  94.0 0.9 copy-start.11
  97.2 2.3 %copy-start.2 = (bf16[64,20,256]{2,0,1:T(8,128)(2,1)S(1)}, bf16[64,20,256]{2,0,1:T(8,128)(2,1)}, u32[]{:S(2)}) copy-start(bf16[64,20,256]{2,0,1:T(8,128)(2,1)} %copy-done.1) | copy-start | bytes 1966084
  98.4 34.9 %copy-start.18 = (bf16[64,256]{1,0:T(8,128)(2,1)S(1)}, bf16[64,256]{1,0:T(8,128)(2,1)}, u32[]{:S(2)}) copy-start(bf16[64,256]{1,0:T(8,128)(2,1)} %copy-done.17) | copy-start | bytes 98308
  98.5 35.1 %copy-start.3 = (bf16[512,256]{1,0:T(8,128)(2,1)S(1)}, bf16[512,256]{1,0:T(8,128)(2,1)}, u32[]{:S(2)}) copy-start(bf16[512,256]{1,0:T(8,128)(2,1)} %param.15) | copy-start | bytes 786436
  98.5 35.1 %copy-start.13 = (bf16[64,256]{1,0:T(8,128)(2,1)S(1)}, bf16[64,256]{1,0:T(8,128)(2,1)}, u32[]{:S(2)}) copy-start(bf16[64,256]{1,0:T(8,128)(2,1)} %copy-done.12) | copy-start | bytes 98308
Sparse Core Ops, SparseCore 0:
  93.4 38.2 all-gather.2

commit v2 on v1

--- a/solution.py
+++ b/solution.py
@@ -1,6 +1,10 @@
+import functools
+
 import jax
 import jax.numpy as jnp
 from jax import lax
+from jax.experimental import pallas as pl
+from jax.experimental.pallas import tpu as pltpu
 from jax.sharding import PartitionSpec as P
 
 gelu_scale = 0.7978845608028654
@@ -20,6 +24,424 @@
 def contract_rows(left, right):
     return lax.dot_general(
         left, right, (((0,), (0,)), ((), ())), preferred_element_type=jnp.float32
+    )
+
+
+def exchange_kernel(
+    axis_count,
+    nbr_count,
+    node_ref,
+    edge_ref,
+    nbr_col_ref,
+    nbr_row_ref,
+    wself_ref,
+    wnbr_ref,
+    wedge_ref,
+    bias_ref,
+    weout_ref,
+    wnout_ref,
+    gnode_ref,
+    gedge_ref,
+    dnode_ref,
+    dedge_ref,
+    dself_ref,
+    dnbr_ref,
+    dein_ref,
+    dbias_ref,
+    deout_ref,
+    dnout_ref,
+    table,
+    picks,
+    picks_t,
+    base_pre,
+    base_msg,
+    pre_buf,
+    msg_buf,
+    self_rep,
+    out_rep,
+    s_buf,
+    s_mid,
+    s_own,
+    s_in,
+    w_buf,
+    w_mid,
+    w_own,
+    w_in,
+    n_buf,
+    n_mid,
+    n_own,
+    n_in,
+    w_all,
+    n_all,
+    pair_send,
+    pair_recv,
+    chip_send,
+    chip_recv,
+    all_send,
+    all_recv,
+):
+    f32, bf16 = jnp.float32, jnp.bfloat16
+    chips = axis_count // 2
+    me = lax.axis_index("res")
+    core = lax.rem(me, 2)
+    chip = lax.div(me, 2)
+    sibling = me + 1 - 2 * core
+    rows, width = node_ref.shape
+    edges = edge_ref.shape[0]
+    nodes_all = rows * axis_count
+    tile = 256
+
+    def peer(step):
+        return lax.rem(me + 2 * step, axis_count)
+
+    def remote(src, dst, send, recv, to):
+        return pltpu.make_async_remote_copy(
+            src_ref=src,
+            dst_ref=dst,
+            send_sem=send,
+            recv_sem=recv,
+            device_id={"res": to},
+            device_id_type=pl.DeviceIdType.MESH,
+        )
+
+    def nt(a, b):
+        return lax.dot_general(a, b, (((1,), (1,)), ((), ())), preferred_element_type=f32)
+
+    def nn(a, b):
+        return jnp.dot(a, b, preferred_element_type=f32)
+
+    def gather_copy(kind, buf, block, slot, to):
+        return remote(
+            buf.at[block], buf.at[block], all_send.at[kind, slot], all_recv.at[kind, block], to
+        )
+
+    def gather_start(kind, buf):
+        def send(step, carry):
+            gather_copy(kind, buf, me, step, peer(step)).start()
+            return carry
+
+        lax.fori_loop(1, chips, send, 0)
+        gather_copy(kind, buf, me, 0, sibling).start()
+
+    def gather_forward(kind, buf):
+        def send(step, carry):
+            block = peer(step)
+            gather_copy(kind, buf, block, step, sibling).wait_recv()
+            gather_copy(kind, buf, block, chips + step - 1, sibling).start()
+            return carry
+
+        lax.fori_loop(1, chips, send, 0)
+
+    def gather_finish(kind, buf):
+        def arrive(step, carry):
+            block = lax.rem(sibling + 2 * step, axis_count)
+            gather_copy(kind, buf, block, 0, sibling).wait_recv()
+            return carry
+
+        lax.fori_loop(0, chips, arrive, 0)
+
+        def sent(slot, carry):
+            gather_copy(kind, buf, me, slot, sibling).wait_send()
+            return carry
+
+        lax.fori_loop(0, 2 * chips - 1, sent, 0)
+
+    def pair_copy(kind, buf, mid):
+        return remote(buf.at[1 - core], mid, pair_send.at[kind], pair_recv.at[kind], sibling)
+
+    def chip_copy(kind, own, into, other):
+        return remote(
+            own.at[other],
+            into.at[chip],
+            chip_send.at[kind, other],
+            chip_recv.at[kind, chip],
+            2 * other + core,
+        )
+
+    def reduce_mid(kind, buf, mid, own, into):
+        pair_copy(kind, buf, mid).wait()
+
+        def add(other, carry):
+            own[other] = (buf[core, other].astype(f32) + mid[other].astype(f32)).astype(bf16)
+            return carry
+
+        lax.fori_loop(0, chips, add, 0)
+
+        def send(step, carry):
+            chip_copy(kind, own, into, lax.rem(chip + step, chips)).start()
+            return carry
+
+        lax.fori_loop(1, chips, send, 0)
+
+    def reduce_end(kind, own, into):
+        into[chip] = own[chip]
+
+        def arrive(step, carry):
+            other = lax.rem(chip + step, chips)
+            remote(
+                own.at[other],
+                into.at[other],
+                chip_send.at[kind, other],
+                chip_recv.at[kind, other],
+                2 * other + core,
+            ).wait()
+            return carry
+
+        lax.fori_loop(1, chips, arrive, 0)
+        total = into[0].astype(f32)
+        for other in range(1, chips):
+            total = total + into[other].astype(f32)
+        return total
+
+    barrier = pltpu.get_barrier_semaphore()
+
+    def greet(step, carry):
+        pl.semaphore_signal(
+            barrier, inc=1, device_id={"res": peer(step)}, device_id_type=pl.DeviceIdType.MESH
+        )
+        return carry
+
+    lax.fori_loop(1, chips, greet, 0)
+    pl.semaphore_signal(
+        barrier, inc=1, device_id={"res": sibling}, device_id_type=pl.DeviceIdType.MESH
+    )
+    table[me] = nn(node_ref[...], wnbr_ref[...]).astype(bf16)
+    pl.semaphore_wait(barrier, chips)
+    gather_start(0, table)
+
+    def split(x):
+        high = x.astype(bf16)
+        return jnp.concatenate([high, (x - high.astype(f32)).astype(bf16)], axis=0)
+
+    self_rep[...] = split(nn(node_ref[...], wself_ref[...]) + bias_ref[...])
+    out_rep[...] = split(nt(gnode_ref[...], wnout_ref[...]) / nbr_count)
+
+    def one_hot(mask):
+        return jnp.where(mask, 1.0, 0.0).astype(bf16)
+
+    def prepare(t, carry):
+        start = pl.multiple_of(t * tile, tile)
+        part = pl.ds(start, tile)
+        picks[part, :] = one_hot(
+            nbr_col_ref[part, :] == lax.broadcasted_iota(jnp.int32, (tile, nodes_all), 1)
+        )
+        row = lax.broadcasted_iota(jnp.int32, (tile, 2 * rows), 0) + start
+        col = lax.broadcasted_iota(jnp.int32, (tile, 2 * rows), 1)
+        first = jnp.where(col >= rows, col - rows, col) * nbr_count
+        rep = one_hot((row >= first) & (row < first + nbr_count))
+        base_pre[part, :] = nn(edge_ref[part, :], wedge_ref[...]) + nn(rep, self_rep[...])
+        base_msg[part, :] = nt(gedge_ref[part, :], weout_ref[...]) + nn(rep, out_rep[...])
+        return carry
+
+    lax.fori_loop(0, edges // tile, prepare, 0)
+
+    def prepare_t(t, carry):
+        start = pl.multiple_of(t * tile, tile)
+        picks_t[pl.ds(start, tile), :] = one_hot(
+            nbr_row_ref[...] == lax.broadcasted_iota(jnp.int32, (tile, edges), 0) + start
+        )
+        return carry
+
+    lax.fori_loop(0, nodes_all // tile, prepare_t, 0)
+    first = lax.broadcasted_iota(jnp.int32, (rows, edges), 0) * nbr_count
+    row = lax.broadcasted_iota(jnp.int32, (rows, edges), 1)
+    own_t = one_hot((row >= first) & (row < first + nbr_count))
+
+    gather_forward(0, table)
+    gather_finish(0, table)
+
+    def middle(t, carry):
+        part = pl.ds(pl.multiple_of(t * tile, tile), tile)
+        preact = base_pre[part, :] + nn(
+            picks[part, :], table[...].reshape(nodes_all, table.shape[2])
+        )
+        values, slopes = gelu_parts(preact)
+        msg_buf[part, :] = values.astype(bf16)
+        pre_buf[part, :] = (base_msg[part, :] * slopes).astype(bf16)
+        return carry
+
+    lax.fori_loop(0, edges // tile, middle, 0)
+
+    def spread(t, carry):
+        part = pl.ds(pl.multiple_of(t * tile, tile), tile)
+        found = nn(picks_t[part, :], pre_buf[...]).astype(bf16)
+        for j in range(tile // rows):
+            s_buf[j % 2, t * (tile // rows // 2) + j // 2] = found[j * rows : (j + 1) * rows]
+        return carry
+
+    lax.fori_loop(0, nodes_all // tile, spread, 0)
+    pair_copy(0, s_buf, s_mid).start()
+
+    pre_sum = nn(own_t, pre_buf[...]).astype(bf16)
+    msg_sum = nn(own_t, msg_buf[...]).astype(bf16)
+
+    def place(buf, at, value):
+        count = value.shape[0] // axis_count
+        for j in range(axis_count):
+            buf[j % 2, j // 2, at : at + count, :] = value[j * count : (j + 1) * count].astype(bf16)
+
+    hid = table.shape[2]
+    own_self = width // axis_count
+    own_hid = hid // axis_count
+    place(w_buf, 0, contract_rows(node_ref[...], pre_sum))
+    place(w_buf, own_self, contract_rows(edge_ref[...], pre_buf[...]))
+    place(w_buf, own_self + own_hid, contract_rows(msg_buf[...], gedge_ref[...]))
+    nout = contract_rows(msg_sum, gnode_ref[...]) / nbr_count
+    place(w_buf, own_self + 2 * own_hid, nout[:, :hid])
+    place(w_buf, own_self + 3 * own_hid, nout[:, hid:])
+    pair_copy(1, w_buf, w_mid).start()
+
+    reduce_mid(0, s_buf, s_mid, s_own, s_in)
+    reduce_mid(1, w_buf, w_mid, w_own, w_in)
+
+    def edge_out(t, carry):
+        part = pl.ds(pl.multiple_of(t * tile, tile), tile)
+        dedge_ref[part, :] = (
+            nt(pre_buf[part, :], wedge_ref[...]) + gedge_ref[part, :].astype(f32)
+        ).astype(bf16)
+        return carry
+
+    lax.fori_loop(0, edges // tile, edge_out, 0)
+
+    reached = reduce_end(0, s_own, s_in)
+    bias_sum = jnp.sum(reached, axis=0, keepdims=True)
+    reached = reached.astype(bf16)
+    place(n_buf, 0, contract_rows(node_ref[...], reached))
+    pair_copy(2, n_buf, n_mid).start()
+    dnode_ref[...] = (
+        nt(pre_sum, wself_ref[...]) + nt(reached, wnbr_ref[...]) + gnode_ref[...].astype(f32)
+    ).astype(bf16)
+    reduce_mid(2, n_buf, n_mid, n_own, n_in)
+
+    count = w_in.shape[1]
+    w_all[me, 0:count, :] = reduce_end(1, w_own, w_in).astype(bf16)
+    high = bias_sum.astype(bf16).astype(f32)
+    line = lax.broadcasted_iota(jnp.int32, (16, hid), 0)
+    w_all[me, count : count + 16, :] = jnp.where(
+        line == 0, high, jnp.where(line == 1, bias_sum - high, 0.0)
+    ).astype(bf16)
+    gather_start(1, w_all)
+    n_all[me] = reduce_end(2, n_own, n_in).astype(bf16)
+    gather_start(2, n_all)
+    gather_forward(1, w_all)
+    gather_forward(2, n_all)
+    gather_finish(1, w_all)
+
+    def unpack(out, buf, at, size, cols):
+        for j in range(axis_count):
+            out[j * size : (j + 1) * size, cols] = buf[j, at : at + size, :]
+
+    unpack(dself_ref, w_all, 0, own_self, slice(0, hid))
+    unpack(dein_ref, w_all, own_self, own_hid, slice(0, hid))
+    unpack(deout_ref, w_all, own_self + own_hid, own_hid, slice(0, hid))
+    unpack(dnout_ref, w_all, own_self + 2 * own_hid, own_hid, slice(0, hid))
+    unpack(dnout_ref, w_all, own_self + 3 * own_hid, own_hid, slice(hid, 2 * hid))
+    total = w_all[0, count : count + 16, :].astype(f32)
+    for j in range(1, axis_count):
+        total = total + w_all[j, count : count + 16, :].astype(f32)
+    dbias_ref[...] = jnp.sum(total, axis=0, keepdims=True)
+    gather_finish(2, n_all)
+    unpack(dnbr_ref, n_all, 0, own_self, slice(0, hid))
+
+
+def fused(
+    node_feats,
+    edge_feats,
+    neighbours,
+    w_self,
+    w_nbr,
+    w_edge,
+    bias,
+    w_edge_out,
+    w_node_out,
+    grad_nodes,
+    grad_edges,
+):
+    rows, nbr_count = neighbours.shape
+    width, hid = w_self.shape
+    edge_width = edge_feats.shape[2]
+    edges = rows * nbr_count
+    blocks = lax.axis_size("res")
+    chips = blocks // 2
+    nodes_all = rows * blocks
+    own_w = (width + edge_width + hid + 2 * hid) // blocks
+    own_n = width // blocks
+    bf16, f32 = jnp.bfloat16, jnp.float32
+    vmem = pl.BlockSpec(memory_space=pltpu.VMEM)
+
+    def reduce_bufs(count):
+        return [
+            pltpu.VMEM((2, chips, count, hid), bf16),
+            pltpu.VMEM((chips, count, hid), bf16),
+            pltpu.VMEM((chips, count, hid), bf16),
+            pltpu.VMEM((chips, count, hid), bf16),
+        ]
+
+    flops = 2 * edges * hid * (2 * nodes_all + 5 * edge_width)
+    outs = pl.pallas_call(
+        functools.partial(exchange_kernel, blocks, nbr_count),
+        out_shape=(
+            jax.ShapeDtypeStruct((rows, width), bf16),
+            jax.ShapeDtypeStruct((edges, edge_width), bf16),
+            jax.ShapeDtypeStruct((width, hid), bf16),
+            jax.ShapeDtypeStruct((width, hid), bf16),
+            jax.ShapeDtypeStruct((edge_width, hid), bf16),
+            jax.ShapeDtypeStruct((1, hid), f32),
+            jax.ShapeDtypeStruct((hid, edge_width), bf16),
+            jax.ShapeDtypeStruct((hid, width), bf16),
+        ),
+        in_specs=[vmem] * 12,
+        out_specs=[vmem] * 8,
+        scratch_shapes=[
+            pltpu.VMEM((blocks, rows, hid), bf16),
+            pltpu.VMEM((edges, nodes_all), bf16),
+            pltpu.VMEM((nodes_all, edges), bf16),
+            pltpu.VMEM((edges, hid), f32),
+            pltpu.VMEM((edges, hid), f32),
+            pltpu.VMEM((edges, hid), bf16),
+            pltpu.VMEM((edges, hid), bf16),
+            pltpu.VMEM((2 * rows, hid), bf16),
+            pltpu.VMEM((2 * rows, hid), bf16),
+            *reduce_bufs(rows),
+            *reduce_bufs(own_w),
+            *reduce_bufs(own_n),
+            pltpu.VMEM((blocks, own_w + 16, hid), bf16),
+            pltpu.VMEM((blocks, own_n, hid), bf16),
+            pltpu.SemaphoreType.DMA((3,)),
+            pltpu.SemaphoreType.DMA((3,)),
+            pltpu.SemaphoreType.DMA((3, chips)),
+            pltpu.SemaphoreType.DMA((3, chips)),
+            pltpu.SemaphoreType.DMA((3, blocks)),
+            pltpu.SemaphoreType.DMA((3, blocks)),
+        ],
+        compiler_params=pltpu.CompilerParams(
+            collective_id=0, has_side_effects=True, vmem_limit_bytes=40 * 1024 * 1024
+        ),
+        cost_estimate=pl.CostEstimate(flops=flops, bytes_accessed=8_000_000, transcendentals=edges * hid),
+    )(
+        node_feats,
+        edge_feats.reshape(edges, edge_width),
+        neighbours.reshape(edges, 1),
+        neighbours.reshape(1, edges),
+        w_self,
+        w_nbr,
+        w_edge,
+        bias.reshape(1, hid),
+        w_edge_out,
+        w_node_out,
+        grad_nodes,
+        grad_edges.reshape(edges, edge_width),
+    )
+    d_nodes, d_edges, d_self, d_nbr, d_ein, d_bias, d_eout, d_nout = outs
+    return (
+        d_nodes,
+        d_edges.reshape(rows, nbr_count, edge_width),
+        d_self,
+        d_nbr,
+        d_ein,
+        d_bias.reshape(hid),
+        d_eout,
+        d_nout,
     )
 
 
@@ -149,4 +571,6 @@
         P(("groups", "feat"), None),
         P(("groups", "feat"), None),
     )
-    return jax.shard_map(local, mesh=mesh, in_specs=in_specs, out_specs=out_specs, check_vma=False)
+    short = mesh.shape["res"] <= 16 and mesh.shape["feat"] == 1
+    body = fused if short else local
+    return jax.shard_map(body, mesh=mesh, in_specs=in_specs, out_specs=out_specs, check_vma=False)

time: 148 us -> 72.7 us (0.49)
  blocking collectives: 86.9 us -> 0 us
  Pallas kernels: 0 us -> 54.2 us
  between operations: 14.5 us -> 0.74 us
  matrix products: 13.7 us -> 0 us
  waiting for transfers between devices: 10.7 us -> 0 us
  starting transfers between devices: 3.61 us -> 0 us
  other arithmetic: 1.68 us -> 0 us
    pallas_call x0 -> x1, Pallas kernels: none -> 54.2 us  [fused(): pl.pallas_call(functools.partial(exchange_kernel, blocks, nbr_count), out...]
    psum x1 -> x0, blocking collectives: 33.7 us -> none  [local(): grad_bias = lax.psum(jnp.sum(pre_flat.astype(jnp.float32), axis=0), 'res')]
    all_to_all x1 -> x0, blocking collectives: 28.7 us -> none  [local(): lax.all_to_all(packed, 'res', split_axis=0, concat_axis=0, tiled=True)]
    all_gather x1 -> x0, blocking collectives: 24.6 us -> none  [local(): table = lax.all_gather(projected, 'res', axis=0, tiled=True)]
    dot_general x15 -> x0, matrix products: 13.7 us -> none  [the longest x6 5.14 us: contract_rows(): lax.dot_general(left, right, (((0,), (0,)), ((), ())), preferred_element_...]
    unnamed x47 -> x39, local copies, waits for them, and re-layouts: 5.8 us -> 16.6 us
    all_to_all x1 -> x0, waiting for transfers between devices: 10.7 us -> none  [local(): lax.all_to_all(spread.reshape(blocks_res, res_rows, hidden), 'res', split...]
    reshape x14 -> x5, local copies, waits for them, and re-layouts: 6.8 us -> 0.73 us  [the longest x1 0.23 us: fused(): neighbours.reshape(edges, 1)]
  transfers between devices with their start and end apart: 2 -> 0, of which waited for: 1 -> 0; matrix products, arithmetic and copies ran while one was open for 6% -> 0% of each run, Pallas kernels for 0% -> 0%
where the time goes in v2:
time: 72.7 us; the launch traced here: 72.2 us
  Pallas kernels  54.2 us (75%)
  local copies, waits for them, and re-layouts  17.3 us (24%)
  between operations  0.74 us (1%)
    pallas_call x1, Pallas kernels, fused(): pl.pallas_call(functools.partial(exchange_kernel, blocks, nbr_count), out...  54.2 us
    unnamed x39, local copies, waits for them, and re-layouts  16.6 us

profile of v2, /device:TPU:0, one launch (start us, length us, event | category | flops | bytes accessed | tf_op | source)
XLA Modules:
  0.0 72.2 jit_solution(8457312886600787504)
XLA Ops:
  0.6 0.0 copy-start.12
  0.6 0.9 %copy.25 = s32[64,20]{1,0:T(8,128)S(1)} copy(s32[64,20]{0,1:T(8,128)} %param.13) | data formatting | bytes 10240 | tf_op args[2]
  1.5 0.1 reshape.39.nbr_row_ref
  1.6 0.2 reshape.44.nbr_col_ref
  1.8 0.0 copy-done.12
  1.9 0.4 copy.24
  2.2 0.0 copy-start.13
  2.2 0.1 reshape.37.edge_ref
  2.4 0.9 %copy-done.13 = bf16[64,20,256]{2,0,1:T(8,128)(2,1)S(1)} copy-done((bf16[64,20,256]{2,0,1:T(8,128)(2,1)S(1)}, bf16[64,20,256]{2,0,1:T(8,128)(2,1)}, u32[]{:S(2)}) %copy-start.13) | copy-done | bytes 655384
  3.3 0.4 copy.27
  3.7 0.0 copy-start.11
  3.7 0.1 reshape.41.gedge_ref
  3.8 0.5 copy-done.11
  4.4 0.0 copy-start.4
  4.4 0.9 %copy-done.4 = bf16[512,256]{1,0:T(8,128)(2,1)S(1)} copy-done((bf16[512,256]{1,0:T(8,128)(2,1)S(1)}, bf16[512,256]{1,0:T(8,128)(2,1)}, u32[]{:S(2)}) %copy-start.4) | copy-done | bytes 262168
  5.3 0.0 copy-start.5
  5.3 0.9 %copy-done.5 = bf16[512,256]{1,0:T(8,128)(2,1)S(1)} copy-done((bf16[512,256]{1,0:T(8,128)(2,1)S(1)}, bf16[512,256]{1,0:T(8,128)(2,1)}, u32[]{:S(2)}) %copy-start.5) | copy-done | bytes 262168
  6.3 0.0 copy-start.6
  6.3 0.9 %copy-done.6 = bf16[256,512]{1,0:T(8,128)(2,1)S(1)} copy-done((bf16[256,512]{1,0:T(8,128)(2,1)S(1)}, bf16[256,512]{1,0:T(8,128)(2,1)}, u32[]{:S(2)}) %copy-start.6) | copy-done | bytes 262168
  7.2 0.0 copy-start.7
  7.2 0.9 %copy-done.7 = bf16[256,256]{1,0:T(8,128)(2,1)S(1)} copy-done((bf16[256,256]{1,0:T(8,128)(2,1)S(1)}, bf16[256,256]{1,0:T(8,128)(2,1)}, u32[]{:S(2)}) %copy-start.7) | copy-done | bytes 131096
  8.1 0.0 copy-start.8
  8.1 0.9 %copy-done.8 = bf16[256,256]{1,0:T(8,128)(2,1)S(1)} copy-done((bf16[256,256]{1,0:T(8,128)(2,1)S(1)}, bf16[256,256]{1,0:T(8,128)(2,1)}, u32[]{:S(2)}) %copy-start.8) | copy-done | bytes 131096
  9.0 0.0 copy-start.9
  9.0 0.8 %copy-done.9 = bf16[64,512]{1,0:T(8,128)(2,1)S(1)} copy-done((bf16[64,512]{1,0:T(8,128)(2,1)S(1)}, bf16[64,512]{1,0:T(8,128)(2,1)}, u32[]{:S(2)}) %copy-start.9) | copy-done | bytes 65560
  9.9 0.0 copy-start.10
  9.9 0.8 %copy-done.10 = bf16[64,512]{1,0:T(8,128)(2,1)S(1)} copy-done((bf16[64,512]{1,0:T(8,128)(2,1)S(1)}, bf16[64,512]{1,0:T(8,128)(2,1)}, u32[]{:S(2)}) %copy-start.10) | copy-done | bytes 65560
  10.7 54.2 %shard_map.170 = (bf16[64,512]{1,0:T(8,128)(2,1)S(1)}, bf16[1280,256]{1,0:T(8,128)(2,1)S(1)}, bf16[512,256]{1,0:T(8,128)(2,1)S(1)}, bf16[512,256]{1,0:T(8,128)(2...) custom-call(bf16[64,512]{1,0:T(8,128)(2,1)S(1)} %copy-done.9, ...), custom_call_target="tpu_custom_call" | custom-call | flops 2181038080 | bytes 8000000 | tf_op jit(solution)/shard_map/pallas_call | solution.py:381
  64.9 0.0 copy-start
  64.9 0.6 copy-done
  65.6 0.0 copy-start.2
  65.6 0.6 copy-done.2
  66.2 0.1 reshape.42
  66.3 0.0 copy-start.3
  66.3 1.0 %copy.29 = bf16[64,20,256]{2,0,1:T(8,128)(2,1)} copy(bf16[64,20,256]{2,1,0:T(8,128)(2,1)S(1)} %reshape.42) | data formatting | bytes 1310720
  67.3 0.0 copy-done.3
  67.3 0.6 copy.37
  68.0 0.7 copy.38
  68.7 0.0 copy-start.1
  68.7 0.7 copy.39
  69.4 0.3 copy-done.1
  69.7 0.7 copy.40
  70.3 0.6 copy.41
  70.9 0.7 copy.42
  71.5 0.7 copy.43
Async XLA Ops:
  0.6 1.2 %copy-start.12 = (bf16[64,20,256]{2,0,1:T(8,128)(2,1)S(1)}, bf16[64,20,256]{2,0,1:T(8,128)(2,1)}, u32[]{:S(2)}) copy-start(bf16[64,20,256]{2,0,1:T(8,128)(2,1)} %param.12) | copy-start | bytes 1966084
  2.2 1.1 %copy-start.13 = (bf16[64,20,256]{2,0,1:T(8,128)(2,1)S(1)}, bf16[64,20,256]{2,0,1:T(8,128)(2,1)}, u32[]{:S(2)}) copy-start(bf16[64,20,256]{2,0,1:T(8,128)(2,1)} %param.21) | copy-start | bytes 1966084
  3.7 0.7 copy-start.11
  4.4 0.9 %copy-start.4 = (bf16[512,256]{1,0:T(8,128)(2,1)S(1)}, bf16[512,256]{1,0:T(8,128)(2,1)}, u32[]{:S(2)}) copy-start(bf16[512,256]{1,0:T(8,128)(2,1)} %wself_ref.1) | copy-start | bytes 786436
  5.3 0.9 %copy-start.5 = (bf16[512,256]{1,0:T(8,128)(2,1)S(1)}, bf16[512,256]{1,0:T(8,128)(2,1)}, u32[]{:S(2)}) copy-start(bf16[512,256]{1,0:T(8,128)(2,1)} %wnbr_ref.1) | copy-start | bytes 786436
  6.3 0.9 %copy-start.6 = (bf16[256,512]{1,0:T(8,128)(2,1)S(1)}, bf16[256,512]{1,0:T(8,128)(2,1)}, u32[]{:S(2)}) copy-start(bf16[256,512]{1,0:T(8,128)(2,1)} %wnout_ref.1) | copy-start | bytes 786436
  7.2 0.9 %copy-start.7 = (bf16[256,256]{1,0:T(8,128)(2,1)S(1)}, bf16[256,256]{1,0:T(8,128)(2,1)}, u32[]{:S(2)}) copy-start(bf16[256,256]{1,0:T(8,128)(2,1)} %wedge_ref.1) | copy-start | bytes 393220
  8.1 0.9 %copy-start.8 = (bf16[256,256]{1,0:T(8,128)(2,1)S(1)}, bf16[256,256]{1,0:T(8,128)(2,1)}, u32[]{:S(2)}) copy-start(bf16[256,256]{1,0:T(8,128)(2,1)} %weout_ref.1) | copy-start | bytes 393220
  9.0 0.8 %copy-start.9 = (bf16[64,512]{1,0:T(8,128)(2,1)S(1)}, bf16[64,512]{1,0:T(8,128)(2,1)}, u32[]{:S(2)}) copy-start(bf16[64,512]{1,0:T(8,128)(2,1)} %node_ref.1) | copy-start | bytes 196612
  9.9 0.8 %copy-start.10 = (bf16[64,512]{1,0:T(8,128)(2,1)S(1)}, bf16[64,512]{1,0:T(8,128)(2,1)}, u32[]{:S(2)}) copy-start(bf16[64,512]{1,0:T(8,128)(2,1)} %gnode_ref.1) | copy-start | bytes 196612
  64.9 0.7 copy-start
  65.6 0.6 copy-start.2
  66.3 1.0 %copy-start.3 = (bf16[64,512]{1,0:T(8,128)(2,1)S(1)}, bf16[64,512]{1,0:T(8,128)(2,1)}, u32[]{:S(2)}) copy-start(bf16[64,512]{1,0:T(8,128)(2,1)} %copy-done.2) | copy-start | bytes 196612
  68.7 1.0 %copy-start.1 = (bf16[256,256]{1,0:T(8,128)(2,1)S(1)}, bf16[256,256]{1,0:T(8,128)(2,1)}, u32[]{:S(2)}) copy-start(bf16[256,256]{1,0:T(8,128)(2,1)} %copy-done) | copy-start | bytes 393220

commit v3 on v2

--- a/solution.py
+++ b/solution.py
@@ -30,18 +30,18 @@
 def exchange_kernel(
     axis_count,
     nbr_count,
-    node_ref,
-    edge_ref,
+    node_hbm,
+    edge_hbm,
     nbr_col_ref,
     nbr_row_ref,
-    wself_ref,
-    wnbr_ref,
-    wedge_ref,
+    wself_hbm,
+    wnbr_hbm,
+    wedge_hbm,
     bias_ref,
-    weout_ref,
-    wnout_ref,
-    gnode_ref,
-    gedge_ref,
+    weout_hbm,
+    wnout_hbm,
+    gnode_hbm,
+    gedge_hbm,
     dnode_ref,
     dedge_ref,
     dself_ref,
@@ -50,6 +50,16 @@
     dbias_ref,
     deout_ref,
     dnout_ref,
+    node_ref,
+    wself_ref,
+    wnbr_ref,
+    wedge_ref,
+    weout_ref,
+    wnout_ref,
+    gnode_ref,
+    edge_ref,
+    gedge_ref,
+    in_sem,
     table,
     picks,
     picks_t,
@@ -115,22 +125,35 @@
             buf.at[block], buf.at[block], all_send.at[kind, slot], all_recv.at[kind, block], to
         )
 
+    across = 4 * lax.div(me, 4) + lax.rem(me + 2, 4)
+    planes = axis_count // 4
+
     def gather_start(kind, buf):
         def send(step, carry):
-            gather_copy(kind, buf, me, step, peer(step)).start()
-            return carry
-
-        lax.fori_loop(1, chips, send, 0)
+            gather_copy(kind, buf, me, step, peer(2 * step)).start()
+            return carry
+
+        lax.fori_loop(1, planes, send, 0)
+        gather_copy(kind, buf, me, planes, across).start()
         gather_copy(kind, buf, me, 0, sibling).start()
 
     def gather_forward(kind, buf):
-        def send(step, carry):
-            block = peer(step)
-            gather_copy(kind, buf, block, step, sibling).wait_recv()
-            gather_copy(kind, buf, block, chips + step - 1, sibling).start()
-            return carry
-
-        lax.fori_loop(1, chips, send, 0)
+        def along(step, carry):
+            block = peer(2 * step)
+            gather_copy(kind, buf, block, 0, sibling).wait_recv()
+            gather_copy(kind, buf, block, planes + step, across).start()
+            gather_copy(kind, buf, block, 2 * planes + step - 1, sibling).start()
+            return carry
+
+        lax.fori_loop(1, planes, along, 0)
+
+        def over(step, carry):
+            block = lax.rem(across + 4 * step, axis_count)
+            gather_copy(kind, buf, block, 0, sibling).wait_recv()
+            gather_copy(kind, buf, block, 3 * planes + step - 1, sibling).start()
+            return carry
+
+        lax.fori_loop(0, planes, over, 0)
 
     def gather_finish(kind, buf):
         def arrive(step, carry):
@@ -193,6 +216,24 @@
             total = total + into[other].astype(f32)
         return total
 
+    loads = [
+        pltpu.make_async_copy(source, target, in_sem.at[slot])
+        for slot, (source, target) in enumerate(
+            [
+                (node_hbm, node_ref),
+                (wnbr_hbm, wnbr_ref),
+                (wself_hbm, wself_ref),
+                (gnode_hbm, gnode_ref),
+                (wnout_hbm, wnout_ref),
+                (wedge_hbm, wedge_ref),
+                (weout_hbm, weout_ref),
+                (edge_hbm, edge_ref),
+                (gedge_hbm, gedge_ref),
+            ]
+        )
+    ]
+    for load in loads:
+        load.start()
     barrier = pltpu.get_barrier_semaphore()
 
     def greet(step, carry):
@@ -205,9 +246,13 @@
     pl.semaphore_signal(
         barrier, inc=1, device_id={"res": sibling}, device_id_type=pl.DeviceIdType.MESH
     )
+    loads[0].wait()
+    loads[1].wait()
     table[me] = nn(node_ref[...], wnbr_ref[...]).astype(bf16)
     pl.semaphore_wait(barrier, chips)
     gather_start(0, table)
+    for load in loads[2:]:
+        load.wait()
 
     def split(x):
         high = x.astype(bf16)
@@ -225,10 +270,9 @@
         picks[part, :] = one_hot(
             nbr_col_ref[part, :] == lax.broadcasted_iota(jnp.int32, (tile, nodes_all), 1)
         )
-        row = lax.broadcasted_iota(jnp.int32, (tile, 2 * rows), 0) + start
+        row = lax.broadcasted_iota(jnp.int32, (tile, 2 * rows), 0)
         col = lax.broadcasted_iota(jnp.int32, (tile, 2 * rows), 1)
-        first = jnp.where(col >= rows, col - rows, col) * nbr_count
-        rep = one_hot((row >= first) & (row < first + nbr_count))
+        rep = one_hot(row & (rows - 1) == col & (rows - 1))
         base_pre[part, :] = nn(edge_ref[part, :], wedge_ref[...]) + nn(rep, self_rep[...])
         base_msg[part, :] = nt(gedge_ref[part, :], weout_ref[...]) + nn(rep, out_rep[...])
         return carry
@@ -243,9 +287,9 @@
         return carry
 
     lax.fori_loop(0, nodes_all // tile, prepare_t, 0)
-    first = lax.broadcasted_iota(jnp.int32, (rows, edges), 0) * nbr_count
-    row = lax.broadcasted_iota(jnp.int32, (rows, edges), 1)
-    own_t = one_hot((row >= first) & (row < first + nbr_count))
+    row = lax.broadcasted_iota(jnp.int32, (rows, edges), 0)
+    col = lax.broadcasted_iota(jnp.int32, (rows, edges), 1)
+    own_t = one_hot(col & (rows - 1) == row)
 
     gather_forward(0, table)
     gather_finish(0, table)
@@ -342,6 +386,18 @@
     dbias_ref[...] = jnp.sum(total, axis=0, keepdims=True)
     gather_finish(2, n_all)
     unpack(dnbr_ref, n_all, 0, own_self, slice(0, hid))
+
+
+def store_kernel(*refs):
+    count = len(refs) // 2
+    sems = refs[-1]
+    copies = [
+        pltpu.make_async_copy(refs[slot], refs[count + slot], sems.at[slot]) for slot in range(count)
+    ]
+    for copy in copies:
+        copy.start()
+    for copy in copies:
+        copy.wait()
 
 
 def fused(
@@ -368,6 +424,7 @@
     own_n = width // blocks
     bf16, f32 = jnp.bfloat16, jnp.float32
     vmem = pl.BlockSpec(memory_space=pltpu.VMEM)
+    hbm = pl.BlockSpec(memory_space=pl.ANY)
 
     def reduce_bufs(count):
         return [
@@ -390,9 +447,19 @@
             jax.ShapeDtypeStruct((hid, edge_width), bf16),
             jax.ShapeDtypeStruct((hid, width), bf16),
         ),
-        in_specs=[vmem] * 12,
+        in_specs=[hbm, hbm, vmem, vmem, hbm, hbm, hbm, vmem, hbm, hbm, hbm, hbm],
         out_specs=[vmem] * 8,
         scratch_shapes=[
+            pltpu.VMEM((rows, width), bf16),
+            pltpu.VMEM((width, hid), bf16),
+            pltpu.VMEM((width, hid), bf16),
+            pltpu.VMEM((edge_width, hid), bf16),
+            pltpu.VMEM((hid, edge_width), bf16),
+            pltpu.VMEM((hid, width), bf16),
+            pltpu.VMEM((rows, width), bf16),
+            pltpu.VMEM((edges, edge_width), bf16),
+            pltpu.VMEM((edges, edge_width), bf16),
+            pltpu.SemaphoreType.DMA((9,)),
             pltpu.VMEM((blocks, rows, hid), bf16),
             pltpu.VMEM((edges, nodes_all), bf16),
             pltpu.VMEM((nodes_all, edges), bf16),
@@ -415,14 +482,14 @@
             pltpu.SemaphoreType.DMA((3, blocks)),
         ],
         compiler_params=pltpu.CompilerParams(
-            collective_id=0, has_side_effects=True, vmem_limit_bytes=40 * 1024 * 1024
+            collective_id=0, has_side_effects=True, vmem_limit_bytes=58 * 1024 * 1024
         ),
         cost_estimate=pl.CostEstimate(flops=flops, bytes_accessed=8_000_000, transcendentals=edges * hid),
     )(
         node_feats,
-        edge_feats.reshape(edges, edge_width),
-        neighbours.reshape(edges, 1),
-        neighbours.reshape(1, edges),
+        edge_feats.transpose(1, 0, 2).reshape(edges, edge_width),
+        neighbours.T.reshape(edges, 1),
+        neighbours.T.reshape(1, edges),
         w_self,
         w_nbr,
         w_edge,
@@ -430,12 +497,21 @@
         w_edge_out,
         w_node_out,
         grad_nodes,
-        grad_edges.reshape(edges, edge_width),
-    )
+        grad_edges.transpose(1, 0, 2).reshape(edges, edge_width),
+    )
+    count = len(outs)
+    outs = pl.pallas_call(
+        store_kernel,
+        out_shape=tuple(jax.ShapeDtypeStruct(x.shape, x.dtype) for x in outs),
+        in_specs=[hbm] * count,
+        out_specs=[hbm] * count,
+        scratch_shapes=[pltpu.SemaphoreType.DMA((count,))],
+        compiler_params=pltpu.CompilerParams(vmem_limit_bytes=58 * 1024 * 1024),
+    )(*outs)
     d_nodes, d_edges, d_self, d_nbr, d_ein, d_bias, d_eout, d_nout = outs
     return (
         d_nodes,
-        d_edges.reshape(rows, nbr_count, edge_width),
+        d_edges.reshape(nbr_count, rows, edge_width).transpose(1, 0, 2),
         d_self,
         d_nbr,
         d_ein,
@@ -571,6 +647,6 @@
         P(("groups", "feat"), None),
         P(("groups", "feat"), None),
     )
-    short = mesh.shape["res"] <= 16 and mesh.shape["feat"] == 1
+    short = mesh.shape["res"] == 16 and mesh.shape["feat"] == 1
     body = fused if short else local
     return jax.shard_map(body, mesh=mesh, in_specs=in_specs, out_specs=out_specs, check_vma=False)

time: 72.7 us -> 113 us (1.55)
  Pallas kernels: 54.2 us -> 109 us
  local copies, waits for them, and re-layouts: 17.3 us -> 2.89 us
    pallas_call x0 -> x1, Pallas kernels: none -> 54.8 us  [fused(): pl.pallas_call(store_kernel, out_shape=tuple((jax.ShapeDtypeStruct(x.shap...]
    unnamed x39 -> x2, local copies, waits for them, and re-layouts: 16.6 us -> 0.01 us
    reshape x5 -> x2, local copies, waits for them, and re-layouts: 0.73 us -> 2.88 us  [the longest x1 1.44 us: fused(): neighbours.T.reshape(edges, 1)]
where the time goes in v3:
time: 113 us; the launch traced here: 112 us
  Pallas kernels  109 us (96%)
  local copies, waits for them, and re-layouts  2.89 us (3%)
    pallas_call x1, Pallas kernels, fused(): pl.pallas_call(store_kernel, out_shape=tuple((jax.ShapeDtypeStruct(x.shap...  54.8 us
    pallas_call x1, Pallas kernels, fused(): pl.pallas_call(functools.partial(exchange_kernel, blocks, nbr_count), out...  53.9 us

profile of v3, /device:TPU:0, one launch (start us, length us, event | category | flops | bytes accessed | tf_op | source)
XLA Modules:
  0.0 112.3 jit_solution(5096071245191420032)
XLA Ops:
  0.6 0.0 copy-start
  0.6 1.4 %reshape.39.nbr_row_ref = s32[1,1280]{1,0:T(1,128)} reshape(s32[20,64]{1,0:T(8,128)} %bitcast.12) | data formatting | bytes 10240 | tf_op jit(solution)/shard_map/reshape | solution.py:492
  2.1 0.0 copy-done
  2.1 1.4 %reshape.44.nbr_col_ref = s32[1280,1]{1,0:T(8,128)} reshape(s32[20,64]{1,0:T(8,128)S(1)} %bitcast.13) | data formatting | bytes 10240 | tf_op jit(solution)/shard_map/reshape | solution.py:491
  3.5 53.9 %shard_map.170 = (bf16[64,512]{1,0:T(8,128)(2,1)}, bf16[1280,256]{1,0:T(8,128)(2,1)}, bf16[512,256]{1,0:T(8,128)(2,1)}, bf16[512,256]{1,0:T(8,128)(2,1)}, bf16[2...) custom-call(bf16[64,512]{1,0:T(8,128)(2,1)} %node_hbm.1, ...), custom_call_target="tpu_custom_call" | custom-call | flops 2181038080 | bytes 8000000 | tf_op jit(solution)/shard_map/pallas_call | solution.py:438
  57.5 54.8 %shard_map.171 = (bf16[64,512]{1,0:T(8,128)(2,1)}, bf16[1280,256]{1,0:T(8,128)(2,1)}, bf16[512,256]{1,0:T(8,128)(2,1)}, bf16[512,256]{1,0:T(8,128)(2,1)}, bf16[2...) custom-call(bf16[64,512]{1,0:T(8,128)(2,1)} %get-tuple-element.24.refs_0_, ...), custom_call_target="tpu_custom_call" | custom-call | tf_op jit(solution)/shard_map/pallas_call | solution.py:503
Async XLA Ops:
  0.6 1.5 %copy-start = (s32[64,20]{0,1:T(8,128)S(1)}, s32[64,20]{0,1:T(8,128)}, u32[]{:S(2)}) copy-start(s32[64,20]{0,1:T(8,128)} %param.13) | copy-start | bytes 15364

commit v4 on v3

--- a/solution.py
+++ b/solution.py
@@ -503,7 +503,7 @@
     outs = pl.pallas_call(
         store_kernel,
         out_shape=tuple(jax.ShapeDtypeStruct(x.shape, x.dtype) for x in outs),
-        in_specs=[hbm] * count,
+        in_specs=[vmem] * count,
         out_specs=[hbm] * count,
         scratch_shapes=[pltpu.SemaphoreType.DMA((count,))],
         compiler_params=pltpu.CompilerParams(vmem_limit_bytes=58 * 1024 * 1024),

time: 113 us -> 61.2 us (0.54)
  Pallas kernels: 109 us -> 56.6 us
    pallas_call x1, Pallas kernels: 54.8 us -> 2.68 us  [fused(): pl.pallas_call(store_kernel, out_shape=tuple((jax.ShapeDtypeStruct(x.shap...]
where the time goes in v4:
time: 61.2 us; the launch traced here: 60.1 us
  Pallas kernels  56.6 us (92%)
  local copies, waits for them, and re-layouts  2.89 us (5%)
  between operations  0.65 us (1%)
    pallas_call x1, Pallas kernels, fused(): pl.pallas_call(functools.partial(exchange_kernel, blocks, nbr_count), out...  53.9 us
    pallas_call x1, Pallas kernels, fused(): pl.pallas_call(store_kernel, out_shape=tuple((jax.ShapeDtypeStruct(x.shap...  2.68 us
    reshape x1, local copies, waits for them, and re-layouts, fused(): neighbours.T.reshape(edges, 1)  1.44 us
    reshape x1, local copies, waits for them, and re-layouts, fused(): neighbours.T.reshape(1, edges)  1.44 us

profile of v4, /device:TPU:0, one launch (start us, length us, event | category | flops | bytes accessed | tf_op | source)
XLA Modules:
  0.0 60.1 jit_solution(879933428807890128)
XLA Ops:
  0.6 0.0 copy-start
  0.6 1.4 %reshape.39.nbr_row_ref = s32[1,1280]{1,0:T(1,128)} reshape(s32[20,64]{1,0:T(8,128)} %bitcast.12) | data formatting | bytes 10240 | tf_op jit(solution)/shard_map/reshape | solution.py:492
  2.1 0.0 copy-done
  2.1 1.4 %reshape.44.nbr_col_ref = s32[1280,1]{1,0:T(8,128)} reshape(s32[20,64]{1,0:T(8,128)S(1)} %bitcast.13) | data formatting | bytes 10240 | tf_op jit(solution)/shard_map/reshape | solution.py:491
  3.5 53.9 %shard_map.170 = (bf16[64,512]{1,0:T(8,128)(2,1)}, bf16[1280,256]{1,0:T(8,128)(2,1)}, bf16[512,256]{1,0:T(8,128)(2,1)}, bf16[512,256]{1,0:T(8,128)(2,1)}, bf16[2...) custom-call(bf16[64,512]{1,0:T(8,128)(2,1)} %node_hbm.1, ...), custom_call_target="tpu_custom_call" | custom-call | flops 2181038080 | bytes 8000000 | tf_op jit(solution)/shard_map/pallas_call | solution.py:438
  57.5 2.7 %shard_map.171 = (bf16[64,512]{1,0:T(8,128)(2,1)}, bf16[1280,256]{1,0:T(8,128)(2,1)}, bf16[512,256]{1,0:T(8,128)(2,1)}, bf16[512,256]{1,0:T(8,128)(2,1)}, bf16[2...) custom-call(bf16[64,512]{1,0:T(8,128)(2,1)} %get-tuple-element.24.refs_0_, ...), custom_call_target="tpu_custom_call" | custom-call | tf_op jit(solution)/shard_map/pallas_call | solution.py:503
Async XLA Ops:
  0.6 1.5 %copy-start = (s32[64,20]{0,1:T(8,128)S(1)}, s32[64,20]{0,1:T(8,128)}, u32[]{:S(2)}) copy-start(s32[64,20]{0,1:T(8,128)} %param.13) | copy-start | bytes 15364
